TPU v7x, 256 devices: a whole 4x4x8 slice. The times are simulated.
256 devices in a mesh: rows: 64 (over x, z, core), cols: 4 (over y).
Axes of the slice: x: 4, y: 4, z: 8, core: 2. Of those that a mesh axis runs over, the one named last changes fastest.
Arguments:
- kernel: float32 [16384, 16384], P('rows', 'cols'), may hold values from 0 to 2, as said below
- row_block: int32 [256], P('rows'), may hold values from 0 to 255, as said below
- panel_order: int32 [2], replicated, may hold values from 0 to 63, as said below
- samples: float32 [16384, 512], P('rows', 'cols'), may hold values from -6 to 6
Outputs:
- trailing: float32 [16384, 16384], P('rows', 'cols')
- factor: float32 [16384, 512], P('rows')
- solved: float32 [512, 512], P(None, 'cols')
- reduced_samples: float32 [16384, 512], P('rows', 'cols')
Inputs may be any that keep to these rules, and one draw needn't show every extreme that they name: `row_block`: the stored row blocks of rows index i (stored blocks i * 4 to (i + 1) * 4 - 1) hold the global row blocks i + t * 64, t = 0 .. 3, each once, in some order. `panel_order`: the entries are distinct, and one of them is 63. `kernel`: in global row order the matrix is symmetric and positive definite, its smallest eigenvalue 0.25 or more.
All inputs are finite; a program needn't handle non-finite values.
Results may differ from a plain program's by a relative error of at most 0.0003.
Values sent between devices are 32-bit elements; how exact they have to be, the bound alone decides.
No kernel may reach another device: no remote copies, remote signals or barrier semaphores. Data moves between devices by JAX's collectives and lax.ppermute only.
A program may use at most 128 MiB of HBM per device.

v0:
```python
import jax
import jax.numpy as jnp
from jax import lax
from jax.sharding import PartitionSpec as P

PW = 256
PANELS = 2


EXACT = lax.Precision.HIGHEST


def broadcast(block, axis, owner):
    block = jnp.where(lax.axis_index(axis) == owner, block, jnp.zeros_like(block))
    return lax.psum(block, axis)


def times_transposed(left_side, right_side):
    return lax.dot_general(
        left_side,
        right_side,
        (((1,), (1,)), ((), ())),
        precision=EXACT,
        preferred_element_type=jnp.float32,
    )


def matmul_plain(left_side, right_side):
    return jnp.dot(left_side, right_side, precision=EXACT, preferred_element_type=jnp.float32)


def stored_order(array, restore, blocks_here):
    width_here = array.shape[1]
    return jnp.take(array.reshape(blocks_here, -1, width_here), restore, axis=0).reshape(
        array.shape
    )


def on_device(kernel, row_block, panel_order, samples):
    rows_count = lax.axis_size("rows")
    cols_count = lax.axis_size("cols")
    cols_place = lax.axis_index("cols")
    blocks_here = row_block.shape[0]
    local_rows, local_cols = kernel.shape
    block_rows = local_rows // blocks_here
    per_panel = PW // block_rows
    share = blocks_here // cols_count
    right_cols = samples.shape[1]
    ranking = jnp.argsort(row_block)
    restore = jnp.argsort(ranking)
    sorted_blocks = jnp.take(row_block, ranking)
    trailing_work = jnp.take(
        kernel.reshape(blocks_here, block_rows, local_cols), ranking, axis=0
    ).reshape(local_rows, local_cols)
    right_side = jnp.take(
        samples.reshape(blocks_here, block_rows, right_cols), ranking, axis=0
    ).reshape(local_rows, right_cols)
    identity = jnp.eye(PW, dtype=jnp.float32)
    factors = []
    solutions = []
    for panel_step in range(PANELS):
        panel_start = panel_order[panel_step] * PW
        column_owner = panel_start // local_cols
        offset = panel_start - column_owner * local_cols
        own_columns = lax.dynamic_slice_in_dim(trailing_work, offset, PW, 1)
        columns = broadcast(own_columns, "cols", column_owner)
        first_block = panel_order[panel_step] * per_panel
        wanted = first_block + jnp.arange(per_panel, dtype=jnp.int32)
        chooser = (wanted[:, None] == sorted_blocks[None, :]).astype(jnp.float32)
        diag_part = jnp.einsum(
            "ot,trp->orp", chooser, columns.reshape(blocks_here, block_rows, PW), precision=EXACT
        ).reshape(PW, PW)
        right_part = jnp.einsum(
            "ot,trp->orp",
            chooser,
            right_side.reshape(blocks_here, block_rows, right_cols),
            precision=EXACT,
        ).reshape(PW, right_cols)
        diagonal, panel_right = lax.psum((diag_part, right_part), "rows")
        lower_factor = jnp.linalg.cholesky(diagonal)
        inverse = jax.scipy.linalg.solve_triangular(lower_factor, identity, lower=True)
        factor_own = times_transposed(columns, inverse)
        solved_now = matmul_plain(inverse, panel_right)
        right_side = right_side - matmul_plain(factor_own, solved_now)
        my_piece = lax.dynamic_slice_in_dim(
            factor_own, cols_place * share * block_rows, share * block_rows, 0
        )
        spread = times_transposed(factor_own, lax.all_gather(my_piece, "rows", axis=0, tiled=True))
        update = (
            spread.reshape(local_rows, rows_count, share, block_rows)
            .transpose(0, 2, 1, 3)
            .reshape(local_rows, local_cols)
        )
        trailing_work = trailing_work - update
        factors.append(factor_own)
        solutions.append(solved_now)
    factor_all = jnp.concatenate(factors, 1)
    return (
        stored_order(trailing_work, restore, blocks_here),
        stored_order(factor_all, restore, blocks_here),
        jnp.concatenate(solutions, 0),
        stored_order(right_side, restore, blocks_here),
    )


def solution(mesh):
    in_specs = (P("rows", "cols"), P("rows"), P(), P("rows", "cols"))
    out_specs = (P("rows", "cols"), P("rows", None), P(None, "cols"), P("rows", "cols"))
    return jax.shard_map(
        on_device, mesh=mesh, in_specs=in_specs, out_specs=out_specs, check_vma=False
    )
```

profile of v0, /device:TPU:1, one launch (start us, length us, event | category | flops | bytes accessed | tf_op | source)
XLA Modules:
  0.0 816.9 jit_solution(4630192233342211881)
XLA Ops:
  7.2 1.3 fusion.51
  9.2 1.4 sort.31
  10.6 1.3 gather_fusion
  11.9 5.0 gather_fusion.2
  16.9 2.7 broadcast_select_fusion.1
  19.6 2.0 copy-done.2
  21.6 0.7 dynamic-slice_select_fusion.1
  24.0 0.7 copy.24
  24.7 46.3 %all-reduce.8.cloned.1.call-done = f32[256,256]{1,0:T(8,128)} async-done(((f32[256,256]{1,0:T(8,128)}), f32[256,256]{1,0:T(8,128)}) %all-reduce.8.cloned.1.call-update) | async-done | bytes 262160 | tf_op jit(solution)/shard_map/psum | solution.py:15
  71.0 1.5 fusion.4
  72.6 0.8 copy.17
  73.6 183.5 %all-reduce.14.cloned.1.call-done = (f32[256,256]{0,1:T(8,128)}, f32[256,128]{1,0:T(8,128)}) async-done(((f32[256,256]{0,1:T(8,128)}, f32[256,128]{1,0:T(8,128)}), (f32[256,256]{0,1:T(8,128)}, f32[256,128]{1,0:T(8,128)})) %all-reduce.14.cloned.1.call-update) | async-done | bytes 393232 | tf_op jit(solution)/shard_map/psum | solution.py:79
  257.1 1.1 copy.18
  258.2 1.0 fusion.1
  259.2 11.7 %cholesky.130 = f32[128,128]{1,0:T(8,128)S(1)} custom-call(f32[128,128]{1,0:T(8,128)S(1)} %cholesky.194), custom_call_target="Cholesky" | custom-call | tf_op jit(solution)/shard_map/jit(cholesky)/cholesky | solution.py:80
  271.0 9.8 %custom-call.13 = f32[1,128,128]{1,2,0:T(8,128)S(1)} custom-call(f32[1,128,128]{2,1,0:T(8,128)S(1)} %get-tuple-element.61), custom_call_target="InvertDiagBlocksLowerTriangular" | custom-call | tf_op jit(solution)/shard_map/jit(cholesky)/cholesky | solution.py:80
  281.3 11.7 %cholesky.147 = f32[128,128]{1,0:T(8,128)S(1)} custom-call(f32[128,128]{1,0:T(8,128)S(1)} %convolution_subtract_fusion.7), custom_call_target="Cholesky" | custom-call | tf_op jit(solution)/shard_map/jit(cholesky)/cholesky | solution.py:80
  293.1 0.6 compare_reduce_fusion.2
  295.1 4.5 while.4
  296.2 1.4 bitcast_dynamic-update-slice_fusion.4
  298.2 1.4 bitcast_dynamic-update-slice_fusion.4
  299.6 19.7 %custom-call.14 = f32[2,128,128]{1,2,0:T(8,128)S(1)} custom-call(f32[2,128,128]{2,1,0:T(8,128)S(1)} %get-tuple-element.26), custom_call_target="InvertDiagBlocksLowerTriangular" | custom-call | tf_op jit(solution)/shard_map/jit(_solve_triangular)/triangular_solve | solution.py:81
  323.1 78.1 %all-gather.3.cloned.1.call-done = f32[4096,256]{1,0:T(8,128)} async-done(((f32[64,256]{1,0:T(8,128)}), f32[4096,256]{1,0:T(8,128)}) %all-gather.3.cloned.1.call-update) | async-done | bytes 4194320 | tf_op jit(solution)/shard_map/all_gather | solution.py:88
  401.1 11.4 %convolution_subtract_fusion.1 = f32[256,4096]{1,0:T(8,128)S(1)} fusion(f32[256,4096]{1,0:T(8,128)} %bitcast.108, f32[256,256]{1,0:T(8,128)S(1)} %fusion.10, f32[4096,256]{1,0:T(8,128)} %all-gather.3.cloned.1.call-done), kind=kOutput, calls=%fused_computation.11 | convolution fusion | flops 3222274048 | bytes 12845056 | tf_op jit(solution)/shard_map/dot_general | solution.py:19
  412.6 2.0 copy-done.1
  414.6 0.7 dynamic-slice_select_fusion
  416.1 0.7 copy.26
  416.8 40.3 %all-reduce.10.cloned.1.call-done = f32[256,256]{1,0:T(8,128)} async-done(((f32[256,256]{1,0:T(8,128)}), f32[256,256]{1,0:T(8,128)}) %all-reduce.10.cloned.1.call-update) | async-done | bytes 262160 | tf_op jit(solution)/shard_map/psum | solution.py:15
  457.1 1.5 fusion.2
  458.7 0.8 copy.21
  459.8 183.3 %all-reduce.12.cloned.1.call-done = (f32[256,256]{0,1:T(8,128)}, f32[256,128]{1,0:T(8,128)}) async-done(((f32[256,256]{0,1:T(8,128)}, f32[256,128]{1,0:T(8,128)}), (f32[256,256]{0,1:T(8,128)}, f32[256,128]{1,0:T(8,128)})) %all-reduce.12.cloned.1.call-update) | async-done | bytes 393232 | tf_op jit(solution)/shard_map/psum | solution.py:79
  643.0 1.1 copy.22
  644.2 1.0 fusion
  645.2 11.7 %cholesky.164 = f32[128,128]{1,0:T(8,128)S(1)} custom-call(f32[128,128]{1,0:T(8,128)S(1)} %cholesky.197), custom_call_target="Cholesky" | custom-call | tf_op jit(solution)/shard_map/jit(cholesky)/cholesky | solution.py:80
  656.9 9.8 %custom-call.15 = f32[1,128,128]{1,2,0:T(8,128)S(1)} custom-call(f32[1,128,128]{2,1,0:T(8,128)S(1)} %get-tuple-element.57), custom_call_target="InvertDiagBlocksLowerTriangular" | custom-call | tf_op jit(solution)/shard_map/jit(cholesky)/cholesky | solution.py:80
  667.2 11.7 %cholesky.181 = f32[128,128]{1,0:T(8,128)S(1)} custom-call(f32[128,128]{1,0:T(8,128)S(1)} %convolution_subtract_fusion.6), custom_call_target="Cholesky" | custom-call | tf_op jit(solution)/shard_map/jit(cholesky)/cholesky | solution.py:80
  681.6 4.2 while.5
  682.4 1.4 bitcast_dynamic-update-slice_fusion.5
  684.4 1.4 bitcast_dynamic-update-slice_fusion.5
  685.8 19.7 %custom-call.16 = f32[2,128,128]{1,2,0:T(8,128)S(1)} custom-call(f32[2,128,128]{2,1,0:T(8,128)S(1)} %get-tuple-element.27), custom_call_target="InvertDiagBlocksLowerTriangular" | custom-call | tf_op jit(solution)/shard_map/jit(_solve_triangular)/triangular_solve | solution.py:81
  707.5 0.7 sort.32
  710.4 0.7 pad_maximum_fusion.3
  711.2 0.7 broadcast_select_fusion.2
  711.9 0.9 bitcast_select_fusion
  712.8 74.6 %all-gather.5.cloned.1.call-done = f32[4096,256]{1,0:T(8,128)} async-done(((f32[64,256]{1,0:T(8,128)}), f32[4096,256]{1,0:T(8,128)}) %all-gather.5.cloned.1.call-update) | async-done | bytes 4194320 | tf_op jit(solution)/shard_map/all_gather | solution.py:88
  787.4 12.7 %convolution_subtract_fusion = f32[256,4096]{1,0:T(8,128)} fusion(f32[256,4096]{1,0:T(8,128)} %copy-done.1, f32[256,256]{1,0:T(8,128)S(1)} %fusion.8, f32[4096,256]{1,0:T(8,128)} %all-gather.5.cloned.1.call-done), kind=kOutput, calls=%fused_computation.10 | convolution fusion | flops 3222274048 | bytes 12845056 | tf_op jit(solution)/shard_map/dot_general | solution.py:19
  800.1 4.9 gather_fusion.3
  805.0 4.8 broadcast_select_fusion
  (88 shorter events, 13.7 us)
Async XLA Ops:
  7.2 15.9 %copy-start = (f32[256,128]{1,0:T(8,128)S(1)}, f32[256,128]{1,0:T(8,128)}, u32[]{:S(2)}) copy-start(f32[256,128]{1,0:T(8,128)} %param.14) | copy-start | bytes 393220
  7.2 63.8 %all-reduce.8.cloned.1.call-start = ((), (), s32[]{:S(2)}) async-start(), calls=%async_computation | async-start | bytes 524288 | tf_op jit(solution)/shard_map/psum | solution.py:15
  19.6 2.0 copy-start.2
  22.4 234.8 %all-reduce.14.cloned.1.call-start = ((), (), s32[]{:S(2)}) async-start(), calls=%async_computation.5 | async-start | bytes 786432 | tf_op jit(solution)/shard_map/psum | solution.py:79
  71.0 249.2 %copy-start.3 = (f32[256,256]{1,0:T(8,128)S(1)}, f32[256,256]{1,0:T(8,128)}, u32[]{:S(2)}) copy-start(f32[256,256]{1,0:T(8,128)} %all-reduce.8.cloned.1.call-done) | copy-start | bytes 786436
  73.5 327.7 %all-gather.3.cloned.1.call-start = ((), (), s32[]{:S(2)}) async-start(), calls=%async_computation.1 | async-start | bytes 4259840 | tf_op jit(solution)/shard_map/all_gather | solution.py:88
  257.1 65.6 %copy-start.5 = (f32[256,128]{1,0:T(8,128)S(1)}, f32[256,128]{1,0:T(8,128)}, u32[]{:S(2)}) copy-start(f32[256,128]{1,0:T(8,128)} %get-tuple-element.47) | copy-start | bytes 393220
  321.3 135.8 %all-reduce.10.cloned.1.call-start = ((), (), s32[]{:S(2)}) async-start(), calls=%async_computation.2 | async-start | bytes 524288 | tf_op jit(solution)/shard_map/psum | solution.py:15
  412.6 2.0 copy-start.1
  415.3 227.7 %all-reduce.12.cloned.1.call-start = ((), (), s32[]{:S(2)}) async-start(), calls=%async_computation.4 | async-start | bytes 786432 | tf_op jit(solution)/shard_map/psum | solution.py:79
  457.1 249.3 %copy-start.4 = (f32[256,256]{1,0:T(8,128)S(1)}, f32[256,256]{1,0:T(8,128)}, u32[]{:S(2)}) copy-start(f32[256,256]{1,0:T(8,128)} %all-reduce.10.cloned.1.call-done) | copy-start | bytes 786436
  459.5 327.8 %all-gather.5.cloned.1.call-start = ((), (), s32[]{:S(2)}) async-start(), calls=%async_computation.3 | async-start | bytes 4259840 | tf_op jit(solution)/shard_map/all_gather | solution.py:88
  643.0 65.4 %copy-start.6 = (f32[256,128]{1,0:T(8,128)S(1)}, f32[256,128]{1,0:T(8,128)}, u32[]{:S(2)}) copy-start(f32[256,128]{1,0:T(8,128)} %get-tuple-element.45) | copy-start | bytes 393220
Sparse Core Ops, SparseCore 0:
  22.5 48.4 all-reduce.7
  75.5 181.5 all-reduce.13
  321.4 79.7 all-gather.2
  415.5 41.5 all-reduce.9
  461.4 181.5 all-reduce.11
  707.6 79.7 all-gather.4
where the time goes:
time: 826 us; the launch traced here: 817 us
  waiting for transfers between devices  606 us (73%)
  other arithmetic  124 us (15%)
  local copies, waits for them, and re-layouts  33.1 us (4%)
  matrix products  32.9 us (4%)
  between operations  20 us (2%)
    psum x2, waiting for transfers between devices, on_device(): diagonal, panel_right = lax.psum((diag_part, right_part), 'rows')  367 us
    all_gather x2, waiting for transfers between devices, on_device(): lax.all_gather(my_piece, 'rows', axis=0, tiled=True)  153 us
    psum x2, waiting for transfers between devices, broadcast(): return lax.psum(block, axis)  86.6 us
    another operation x13, other arithmetic, on_device(): lower_factor = jnp.linalg.cholesky(diagonal)  68.5 us
    another operation x5, other arithmetic, on_device(): jax.scipy.linalg.solve_triangular(lower_factor, identity, lower=True)  39.4 us
    dot_general x4, matrix products, times_transposed(): lax.dot_general(left_side, right_side, (((1,), (1,)), ((), ())), precisio...  25 us
  transfers between devices with their start and end apart: 6, of which 6 were waited for; matrix products, arithmetic and copies ran while one was open for 1% of the time, Pallas kernels for 0%

commit v1 on v0

v1 whole, which is shorter than its diff:
```python
import jax
import jax.numpy as jnp
from jax import lax
from jax.experimental import pallas as pl
from jax.experimental.pallas import tpu as pltpu
from jax.sharding import PartitionSpec as P

PW = 256
PANELS = 2
EXACT = lax.Precision.HIGHEST
SIDE = 128
STEP = 8


def dot_nt(a, b, precision=EXACT):
    return lax.dot_general(a, b, (((1,), (1,)), ((), ())), precision=precision, preferred_element_type=jnp.float32)


def dot_nn(a, b, precision=EXACT):
    return lax.dot_general(a, b, (((1,), (0,)), ((), ())), precision=precision, preferred_element_type=jnp.float32)


def lanes_of(rows, lane):
    return jnp.broadcast_to(rows[:, lane : lane + 1], (STEP, SIDE))


def sublanes_of(rows, sub):
    return jnp.broadcast_to(rows[sub : sub + 1, :], (STEP, SIDE))


def small_inverse(spread):
    inv, low = [None] * STEP, [[None] * STEP for _ in range(STEP)]
    rest = [list(r) for r in spread]
    for s in range(STEP):
        inv[s] = lax.rsqrt(rest[s][s])
        for r in range(s + 1, STEP):
            low[r][s] = rest[r][s] * inv[s]
        for r in range(s + 1, STEP):
            for q in range(s + 1, r + 1):
                rest[r][q] = rest[r][q] - low[r][s] * low[q][s]
    out = [[None] * STEP for _ in range(STEP)]
    for r in range(STEP):
        out[r][r] = inv[r]
        for s in range(r):
            total = low[r][s] * out[s][s]
            for q in range(s + 1, r):
                total = total + low[r][q] * out[q][s]
            out[r][s] = -inv[r] * total
    return out


def tile_inverse(d_ref, x_ref):
    groups = SIDE // STEP
    sub = lax.broadcasted_iota(jnp.int32, (STEP, SIDE), 0)
    lane = lax.broadcasted_iota(jnp.int32, (STEP, SIDE), 1)
    left = [d_ref[STEP * g : STEP * (g + 1), :] for g in range(groups)]
    right = [jnp.where(lane == sub + STEP * g, 1.0, 0.0).astype(jnp.float32) for g in range(groups)]
    for b in range(groups):
        here_l, here_r = left[b], right[b]
        cols = [lanes_of(here_l, STEP * b + s) for s in range(STEP)]
        spread = [[sublanes_of(cols[s], r) if s <= r else None for s in range(STEP)] for r in range(STEP)]
        v = small_inverse(spread)
        in_l = [sublanes_of(here_l, s) for s in range(STEP)]
        in_r = [sublanes_of(here_r, s) for s in range(STEP)]
        out_l, out_r = [], []
        for r in range(STEP):
            tl, tr = v[r][0] * in_l[0], v[r][0] * in_r[0]
            for s in range(1, r + 1):
                tl, tr = tl + v[r][s] * in_l[s], tr + v[r][s] * in_r[s]
            out_l.append(tl)
            out_r.append(tr)
        new_r = out_r[0]
        for r in range(1, STEP):
            new_r = jnp.where(sub == r, out_r[r], new_r)
        x_ref[STEP * b : STEP * (b + 1), :] = new_r
        if b + 1 == groups:
            break
        t_l, t_r = [], []
        for s in range(STEP):
            tl, tr = v[STEP - 1][s] * out_l[STEP - 1], v[STEP - 1][s] * out_r[STEP - 1]
            for r in range(s, STEP - 1):
                tl, tr = tl + v[r][s] * out_l[r], tr + v[r][s] * out_r[r]
            t_l.append(tl)
            t_r.append(tr)
        for g in range(b + 1, groups):
            c = [lanes_of(left[g], STEP * b + s) for s in range(STEP)]
            sl, sr = c[0] * t_l[0], c[0] * t_r[0]
            for s in range(1, STEP):
                sl, sr = sl + c[s] * t_l[s], sr + c[s] * t_r[s]
            left[g], right[g] = left[g] - sl, right[g] - sr


def factor_kernel(a_ref, p_ref, rc_ref, ri_ref, f_ref, w_ref, y_ref, r_ref, a, v, d, x):
    size = a.shape[0]
    tiles = size // SIDE
    a[...] = a_ref[...]
    v[...] = jnp.zeros_like(v)

    @pl.loop(0, tiles)
    def _(k):
        at = pl.multiple_of(k * SIDE, SIDE)
        d[...] = a[pl.ds(at, SIDE), pl.ds(at, SIDE)]
        tile_inverse(d, x)
        for step in range(tiles):
            @pl.when(k == step)
            def _():
                lo, hi = step * SIDE, (step + 1) * SIDE
                own = x[...]
                v[lo:hi, lo:hi] = own
                if step:
                    v[lo:hi, :lo] = dot_nn(own, v[lo:hi, :lo])
                if hi < size:
                    below = dot_nt(a[hi:, lo:hi], own)
                    a[hi:, hi:] = a[hi:, hi:] - dot_nt(below, below)
                    v[hi:, :hi] = v[hi:, :hi] - dot_nn(below, v[lo:hi, :hi])

    f = dot_nt(p_ref[...], v[...])
    f_ref[...] = f
    y = dot_nn(v[...], rc_ref[...])
    y_ref[...] = y
    r_ref[...] = ri_ref[...] - dot_nn(f, y)
    w_ref[...] = dot_nn(f, v[...])


def factor_call(a, p, rc, ri):
    size, rows, right = a.shape[0], p.shape[0], rc.shape[1]
    f32 = jnp.float32
    return pl.pallas_call(
        factor_kernel,
        out_shape=[
            jax.ShapeDtypeStruct((rows, size), f32),
            jax.ShapeDtypeStruct((rows, size), f32),
            jax.ShapeDtypeStruct((size, right), f32),
            jax.ShapeDtypeStruct((rows, right), f32),
        ],
        scratch_shapes=[
            pltpu.VMEM((size, size), f32),
            pltpu.VMEM((size, size), f32),
            pltpu.VMEM((SIDE, SIDE), f32),
            pltpu.VMEM((SIDE, SIDE), f32),
        ],
        compiler_params=pltpu.CompilerParams(vmem_limit_bytes=40 * 1024 * 1024),
        name="factor",
    )(a, p, rc, ri)


def pick(choices, index):
    out = choices[0]
    for at in range(1, len(choices)):
        out = jnp.where(index == at, choices[at], out)
    return out


def on_device(kernel, row_block, panel_order, samples):
    rows_count, cols_count = lax.axis_size("rows"), lax.axis_size("cols")
    row_place, col_place = lax.axis_index("rows"), lax.axis_index("cols")
    blocks_here = row_block.shape[0]
    local_rows, local_cols = kernel.shape
    block_rows = local_rows // blocks_here
    right_cols = samples.shape[1]
    part_rows = block_rows // cols_count
    chunks = PANELS * PW // SIDE

    strata = row_block // rows_count
    slots = [
        jnp.sum(jnp.where(strata == t, jnp.arange(blocks_here, dtype=jnp.int32), 0))
        for t in range(blocks_here)
    ]
    slots = jnp.stack(slots)
    owners, x_at, z_at, own = [], [], [], []
    for k in range(PANELS):
        panel = panel_order[k]
        owner = panel * PW // local_cols
        inside = panel % (local_cols // PW)
        owners.append(owner)
        x_at.append(inside // 4)
        z_at.append(inside % 4)
        own.append(lax.dynamic_slice_in_dim(kernel, inside * PW, PW, 1))
    own = jnp.concatenate(own, 1)

    def message(to):
        parts = [lax.dynamic_slice_in_dim(own, slots[to] * block_rows, block_rows, 0)]
        for k in range(PANELS):
            parts.append(
                lax.dynamic_slice_in_dim(
                    own, slots[owners[k]] * block_rows + to * part_rows, part_rows, 0
                )
            )
        return jnp.concatenate(parts, 0)

    def col_ring(shift):
        return [(i, (i + shift) % cols_count) for i in range(cols_count)]

    got = []
    for shift in range(cols_count):
        sent = message((col_place + shift) % cols_count)
        got.append(lax.ppermute(sent, "cols", col_ring(shift)) if shift else sent)
    mine = jnp.concatenate(
        [
            pick([g[:, k * PW : (k + 1) * PW] for g in got], (col_place - owners[k]) % cols_count)
            for k in range(PANELS)
        ],
        1,
    )
    piece = mine[:block_rows]
    across = lax.all_gather(piece, "rows", axis=0, tiled=True)

    load = []
    for k in range(PANELS):
        share = mine[block_rows + k * part_rows : block_rows + (k + 1) * part_rows]
        load += [share[:, c * SIDE : (c + 1) * SIDE] for c in range(chunks)]
        load.append(lax.dynamic_slice_in_dim(samples, slots[owners[k]] * block_rows, block_rows, 0))
    load = jnp.concatenate(load, 0).reshape(PANELS, 2 * block_rows, SIDE)

    def row_pairs(move):
        pairs = []
        for r in range(rows_count):
            x, z, core = move(r // 16, r % 16 // 2, r % 2)
            pairs.append((r, x % 4 * 16 + z % 8 * 2 + core))
        return pairs

    def spread(load, pairs_of, place, at):
        came = [load] + [lax.ppermute(load, "rows", pairs_of(s)) for s in range(1, 4)]
        return jnp.stack([pick([c[k] for c in came], (place - at[k]) % 4) for k in range(PANELS)])

    load = spread(load, lambda s: row_pairs(lambda x, z, c: (x + s, z, c)), row_place // 16, x_at)
    load = spread(
        load, lambda s: row_pairs(lambda x, z, c: (x, z + 2 * s, c)), row_place % 16 // 4, z_at
    )
    other = lax.ppermute(load, "rows", row_pairs(lambda x, z, c: (x, z ^ 1, c)))
    odd = row_place // 2 % 2 == 1
    load = jnp.stack([jnp.where(odd, other, load), jnp.where(odd, load, other)])
    square, right = load[:, :, :block_rows], load[:, :, block_rows:]
    came = [square] + [lax.ppermute(square, "cols", col_ring(s)) for s in range(1, cols_count)]
    square = [pick(came, (col_place - to) % cols_count) for to in range(cols_count)]
    load = jnp.stack(square + [right])
    other = lax.ppermute(load, "rows", row_pairs(lambda x, z, c: (x, z, c ^ 1)))
    odd = row_place % 2 == 1
    load = jnp.stack([jnp.where(odd, other, load), jnp.where(odd, load, other)])
    right = load[:, cols_count].transpose(2, 1, 0, 3, 4).reshape(PANELS * PW, right_cols)
    square = load[:, :cols_count].reshape(2, cols_count, 2, PANELS, chunks, part_rows, SIDE)
    square = square.transpose(3, 2, 0, 1, 5, 4, 6).reshape(PANELS * PW, PANELS * PW)

    came = [piece] + [lax.ppermute(piece, "cols", col_ring(s)) for s in range(1, cols_count)]
    here = jnp.concatenate(
        [pick(came, (col_place - strata[u]) % cols_count) for u in range(blocks_here)], 0
    )
    factor, weights, solved, reduced = factor_call(square, here, right, samples)
    trailing = kernel - dot_nt(weights, across, lax.Precision.HIGH)
    return trailing, factor, solved, reduced


def solution(mesh):
    in_specs = (P("rows", "cols"), P("rows"), P(), P("rows", "cols"))
    out_specs = (P("rows", "cols"), P("rows", None), P(None, "cols"), P("rows", "cols"))
    return jax.shard_map(
        on_device, mesh=mesh, in_specs=in_specs, out_specs=out_specs, check_vma=False
    )
```

time: 826 us -> 148 us (0.18); the launches traced: 817 us -> 148 us
  waiting for transfers between devices: 606 us -> 38 us
  other arithmetic: 124 us -> 5.51 us
  starting transfers between devices: 0.42 us -> 33.6 us
  local copies, waits for them, and re-layouts: 33.1 us -> 4.25 us
  Pallas kernels: 0 us -> 26.3 us
  matrix products: 32.9 us -> 13.9 us
    psum x4 -> x0, waiting for transfers between devices: 453 us -> none  [the longest x2 367 us: on_device(): diagonal, panel_right = lax.psum((diag_part, right_part), 'rows')]
    all_gather x2 -> x1, waiting for transfers between devices: 153 us -> 4.34 us  [on_device(): across = lax.all_gather(piece, 'rows', axis=0, tiled=True)]
    another operation x18 -> x8, other arithmetic: 108 us -> 2.99 us  [the longest x1 2.66 us: on_device(): slots = jnp.stack(slots)]
    ppermute x0 -> x17, waiting for transfers between devices: none -> 33.6 us  [the longest x6 13.7 us: spread(): lax.ppermute(load, 'rows', pairs_of(s))]
    ppermute x0 -> x17, starting transfers between devices: none -> 33.6 us  [the longest x6 15.5 us: spread(): lax.ppermute(load, 'rows', pairs_of(s))]
    pallas_call x0 -> x1, Pallas kernels: none -> 26.3 us  [factor_call(): pl.pallas_call(factor_kernel, out_shape=[jax.ShapeDtypeStruct((rows, size...]
    dot_general x12 -> x1, matrix products: 30.2 us -> 13.9 us  [dot_nt(): lax.dot_general(a, b, (((1,), (1,)), ((), ())), precision=precision, pref...]
    gather x6 -> x0, local copies, waits for them, and re-layouts: 12.9 us -> none  [the longest x3 6.07 us: stored_order(): jnp.take(array.reshape(blocks_here, -1, width_here), restore, axis=0)]
  transfers between devices with their start and end apart: 6 -> 18, of which waited for: 6 -> 13; matrix products, arithmetic and copies ran while one was open for 1% -> 1% of each run, Pallas kernels for 0% -> 18%
where the time goes in v1:
time: 148 us
  waiting for transfers between devices  38 us (26%)
  starting transfers between devices  33.6 us (23%)
  Pallas kernels  26.3 us (18%)
  between operations  26.3 us (18%)
  matrix products  13.9 us (9%)
  other arithmetic  5.51 us (4%)
  local copies, waits for them, and re-layouts  4.25 us (3%)
    pallas_call x1, Pallas kernels, factor_call(): pl.pallas_call(factor_kernel, out_shape=[jax.ShapeDtypeStruct((rows, size...  26.3 us
    ppermute x6, starting transfers between devices, spread(): lax.ppermute(load, 'rows', pairs_of(s))  15.5 us
    dot_general x1, matrix products, dot_nt(): lax.dot_general(a, b, (((1,), (1,)), ((), ())), precision=precision, pref...  13.9 us
    ppermute x6, waiting for transfers between devices, spread(): lax.ppermute(load, 'rows', pairs_of(s))  13.7 us
    ppermute x3, waiting for transfers between devices, on_device(): got.append(lax.ppermute(sent, 'cols', col_ring(shift)) if shift else sent)  7.23 us
    ppermute x3, starting transfers between devices, on_device(): lax.ppermute(square, 'cols', col_ring(s))  6.19 us
    ppermute x3, starting transfers between devices, on_device(): got.append(lax.ppermute(sent, 'cols', col_ring(shift)) if shift else sent)  6.06 us
    ppermute x3, waiting for transfers between devices, on_device(): lax.ppermute(square, 'cols', col_ring(s))  4.94 us
  transfers between devices with their start and end apart: 18, of which 13 were waited for; matrix products, arithmetic and copies ran while one was open for 1% of the time, Pallas kernels for 18%

profile of v1, /device:TPU:1, one launch (start us, length us, event | category | flops | bytes accessed | tf_op | source)
XLA Modules:
  0.0 147.7 jit_solution(13963074589109881099)
XLA Ops:
  7.2 0.0 all-gather.2.cloned.1.call-start
  7.3 1.3 fusion.35
  13.8 1.3 fusion.29
  15.2 2.7 %pad_add_fusion = s32[4]{0:T(128)S(1)} fusion(s32[1]{0:T(128)} %bitcast.5, s32[1]{0:T(128)} %bitcast.4, s32[1]{0:T(128)} %bitcast.3, s32[1]{0:T(128)} %bitcast.2), kind=kLoop, calls=%fused_computation.121 | loop fusion | flops 12 | bytes 32 | tf_op jit(solution)/shard_map/stack | solution.py:169
  17.8 0.7 fusion.34
  22.5 1.1 constant_dynamic-slice_fusion
  23.6 0.1 fusion.3
  23.7 2.2 %collective-permute-start.2 = (f32[96,512]{1,0:T(8,128)S(1)}, f32[96,512]{1,0:T(8,128)S(1)}, u32[]{:S(2)}, u32[]{:S(2)}) collective-permute-start(f32[96,512]{1,0:T(8,128)S(1)} %pad_maximum_fusion.4), channel_id=1, source_target_pairs={{0,1},{1,2},{2,3},{3,0},{4,5},{5,6},{6,7},{7,4},{8,9},{9,10},{10,1... | collective-permute-start | bytes 589832 | tf_op jit(solution)/shard_map/ppermute | solution.py:197
  25.9 2.7 %collective-permute-start.1 = (f32[96,512]{1,0:T(8,128)S(1)}, f32[96,512]{1,0:T(8,128)S(1)}, u32[]{:S(2)}, u32[]{:S(2)}) collective-permute-start(f32[96,512]{1,0:T(8,128)S(1)} %pad_maximum_fusion.3), channel_id=1, source_target_pairs={{0,2},{1,3},{2,0},{3,1},{4,6},{5,7},{6,4},{7,5},{8,10},{9,11},{10,... | collective-permute-start | bytes 589832 | tf_op jit(solution)/shard_map/ppermute | solution.py:197
  28.6 1.1 collective-permute-start
  29.8 0.6 collective-permute-done.2
  30.4 6.6 %collective-permute-done.1 = f32[96,512]{1,0:T(8,128)S(1)} collective-permute-done((f32[96,512]{1,0:T(8,128)S(1)}, f32[96,512]{1,0:T(8,128)S(1)}, u32[]{:S(2)}, u32[]{:S(2)}) %collective-permute-start.1) | collective-permute-done | bytes 196640 | tf_op jit(solution)/shard_map/ppermute | solution.py:197
  37.0 0.0 collective-permute-done
  37.0 0.1 fusion.10
  37.1 0.7 pad_maximum_fusion.6
  37.8 0.0 all-gather.2.cloned.1.call-update
  38.0 1.3 collective-permute-start.5
  39.3 2.5 %collective-permute-start.4 = (f32[2,128,128]{2,1,0:T(8,128)S(1)}, f32[2,128,128]{2,1,0:T(8,128)S(1)}, u32[]{:S(2)}, u32[]{:S(2)}) collective-permute-start(f32[2,128,128]{2,1,0:T(8,128)S(1)} %bitcast.60), channel_id=1, source_target_pairs={{0,128},{4,132},{8,136},{12,140},{16,144},{20,148},{24,152},{28,15... | collective-permute-start | bytes 393224 | tf_op jit(solution)/shard_map/ppermute | solution.py:223
  41.7 1.2 collective-permute-start.3
  42.9 0.2 collective-permute-done.5
  43.1 3.1 %collective-permute-done.4 = f32[2,128,128]{2,1,0:T(8,128)S(1)} collective-permute-done((f32[2,128,128]{2,1,0:T(8,128)S(1)}, f32[2,128,128]{2,1,0:T(8,128)S(1)}, u32[]{:S(2)}, u32[]{:S(2)}) %collective-permute-start.4) | collective-permute-done | bytes 131104 | tf_op jit(solution)/shard_map/ppermute | solution.py:223
  46.2 0.6 collective-permute-done.3
  46.8 3.1 %collective-permute-start.8 = (f32[2,128,128]{2,1,0:T(8,128)S(1)}, f32[2,128,128]{2,1,0:T(8,128)S(1)}, u32[]{:S(2)}, u32[]{:S(2)}) collective-permute-start(f32[2,128,128]{2,1,0:T(8,128)S(1)} %pad_maximum_fusion.8), channel_id=1, source_target_pairs={{0,16},{4,20},{8,24},{12,28},{16,32},{20,36},{24,40},{28,44},{32,4... | collective-permute-start | bytes 393224 | tf_op jit(solution)/shard_map/ppermute | solution.py:223
  49.9 5.1 %collective-permute-start.7 = (f32[2,128,128]{2,1,0:T(8,128)S(1)}, f32[2,128,128]{2,1,0:T(8,128)S(1)}, u32[]{:S(2)}, u32[]{:S(2)}) collective-permute-start(f32[2,128,128]{2,1,0:T(8,128)S(1)} %pad_maximum_fusion.8), channel_id=1, source_target_pairs={{0,32},{4,36},{8,40},{12,44},{16,48},{20,52},{24,56},{28,60},{32,0... | collective-permute-start | bytes 393224 | tf_op jit(solution)/shard_map/ppermute | solution.py:223
  55.0 2.4 %collective-permute-start.6 = (f32[2,128,128]{2,1,0:T(8,128)S(1)}, f32[2,128,128]{2,1,0:T(8,128)S(1)}, u32[]{:S(2)}, u32[]{:S(2)}) collective-permute-start(f32[2,128,128]{2,1,0:T(8,128)S(1)} %pad_maximum_fusion.8), channel_id=1, source_target_pairs={{0,48},{4,52},{8,56},{12,60},{16,0},{20,4},{24,8},{28,12},{32,16},... | collective-permute-start | bytes 393224 | tf_op jit(solution)/shard_map/ppermute | solution.py:223
  57.4 0.0 collective-permute-done.8
  57.4 5.3 %collective-permute-done.7 = f32[2,128,128]{2,1,0:T(8,128)S(1)} collective-permute-done((f32[2,128,128]{2,1,0:T(8,128)S(1)}, f32[2,128,128]{2,1,0:T(8,128)S(1)}, u32[]{:S(2)}, u32[]{:S(2)}) %collective-permute-start.7) | collective-permute-done | bytes 131104 | tf_op jit(solution)/shard_map/ppermute | solution.py:223
  62.7 4.5 %collective-permute-done.6 = f32[2,128,128]{2,1,0:T(8,128)S(1)} collective-permute-done((f32[2,128,128]{2,1,0:T(8,128)S(1)}, f32[2,128,128]{2,1,0:T(8,128)S(1)}, u32[]{:S(2)}, u32[]{:S(2)}) %collective-permute-start.6) | collective-permute-done | bytes 131104 | tf_op jit(solution)/shard_map/ppermute | solution.py:223
  67.2 0.1 collective-permute-start.9
  67.4 4.8 %collective-permute-done.9 = f32[2,128,128]{2,1,0:T(8,128)S(1)} collective-permute-done((f32[2,128,128]{2,1,0:T(8,128)S(1)}, f32[2,128,128]{2,1,0:T(8,128)S(1)}, u32[]{:S(2)}, u32[]{:S(2)}) %collective-permute-start.9) | collective-permute-done | bytes 131104 | tf_op jit(solution)/shard_map/ppermute | solution.py:230
  72.2 2.6 %collective-permute-start.12 = (f32[2,2,64,128]{3,2,1,0:T(8,128)S(1)}, f32[2,2,64,128]{3,2,1,0:T(8,128)S(1)}, u32[]{:S(2)}, u32[]{:S(2)}) collective-permute-start(f32[2,2,64,128]{3,2,1,0:T(8,128)S(1)} %fusion.2), channel_id=1, source_target_pairs={{0,1},{1,2},{2,3},{3,0},{4,5},{5,6},{6,7},{7,4},{8,9},{9,10},{10,1... | collective-permute-start | bytes 393224 | tf_op jit(solution)/shard_map/ppermute | solution.py:234
  74.9 3.5 %collective-permute-start.11 = (f32[2,2,64,128]{3,2,1,0:T(8,128)S(1)}, f32[2,2,64,128]{3,2,1,0:T(8,128)S(1)}, u32[]{:S(2)}, u32[]{:S(2)}) collective-permute-start(f32[2,2,64,128]{3,2,1,0:T(8,128)S(1)} %fusion.2), channel_id=1, source_target_pairs={{0,2},{1,3},{2,0},{3,1},{4,6},{5,7},{6,4},{7,5},{8,10},{9,11},{10,... | collective-permute-start | bytes 393224 | tf_op jit(solution)/shard_map/ppermute | solution.py:234
  78.4 1.2 collective-permute-done.12
  79.6 3.1 %collective-permute-done.11 = f32[2,2,64,128]{3,2,1,0:T(8,128)S(1)} collective-permute-done((f32[2,2,64,128]{3,2,1,0:T(8,128)S(1)}, f32[2,2,64,128]{3,2,1,0:T(8,128)S(1)}, u32[]{:S(2)}, u32[]{:S(2)}) %collective-permute-start.11) | collective-permute-done | bytes 131104 | tf_op jit(solution)/shard_map/ppermute | solution.py:234
  82.7 0.7 collective-permute-done.10
  83.5 2.5 %collective-permute-start.13 = (f32[5,2,2,64,128]{4,3,2,1,0:T(8,128)S(1)}, f32[5,2,2,64,128]{4,3,2,1,0:T(8,128)S(1)}, u32[]{:S(2)}, u32[]{:S(2)}) collective-permute-start(f32[5,2,2,64,128]{4,3,2,1,0:T(8,128)S(1)} %fusion.8), channel_id=1, source_target_pairs={{0,4},{4,0},{8,12},{12,8},{16,20},{20,16},{24,28},{28,24},{32,36},... | collective-permute-start | bytes 1966088 | tf_op jit(solution)/shard_map/ppermute | solution.py:237
  86.0 3.0 %collective-permute-start.15 = (f32[64,512]{1,0:T(8,128)S(1)}, f32[64,512]{1,0:T(8,128)S(1)}, u32[]{:S(2)}, u32[]{:S(2)}) collective-permute-start(f32[64,512]{1,0:T(8,128)S(1)} %copy-done.1), channel_id=1, source_target_pairs={{0,2},{1,3},{2,0},{3,1},{4,6},{5,7},{6,4},{7,5},{8,10},{9,11},{10,... | collective-permute-start | bytes 393224 | tf_op jit(solution)/shard_map/ppermute | solution.py:244
  89.0 0.3 collective-permute-start.14
  89.3 0.6 fusion.33
  92.5 2.9 %collective-permute-done.15 = f32[64,512]{1,0:T(8,128)S(1)} collective-permute-done((f32[64,512]{1,0:T(8,128)S(1)}, f32[64,512]{1,0:T(8,128)S(1)}, u32[]{:S(2)}, u32[]{:S(2)}) %collective-permute-start.15) | collective-permute-done | bytes 131104 | tf_op jit(solution)/shard_map/ppermute | solution.py:244
  95.4 0.1 select_select_fusion.3
  95.5 0.2 select_bitcast_fusion
  95.7 0.1 fusion
  95.8 0.4 copy.8
  96.3 0.1 copy.12
  96.4 26.3 %factor.1 = (f32[256,512]{1,0:T(8,128)}, f32[256,512]{1,0:T(8,128)S(1)}, f32[512,128]{1,0:T(8,128)}, f32[256,128]{1,0:T(8,128)}) custom-call(f32[512,512]{1,0:T(8,128)S(1)} %bitcast.55, f32[256,512]{1,0:T(8,128)S(1)} %pad_maximum_fusion.p_ref, f32[512,128]{1,0:T(8,128)S(1)} %bitcast.56, f32[256,128]{1,0:T(8,128)S(1)} %copy-done), custom_call_target="tpu_custom_call" | custom-call | tf_op jit(solution)/shard_map/factor/pallas_call | solution.py:128
  122.7 4.3 %all-gather.2.cloned.1.call-done = f32[4096,512]{1,0:T(8,128)} async-done(((f32[64,512]{1,0:T(8,128)}), f32[4096,512]{1,0:T(8,128)}) %all-gather.2.cloned.1.call-update) | async-done | bytes 8388624 | tf_op jit(solution)/shard_map/all_gather | solution.py:206
  127.1 13.9 %convolution_subtract_fusion = f32[256,4096]{1,0:T(8,128)} fusion(f32[256,4096]{1,0:T(8,128)} %param.4, f32[256,512]{1,0:T(8,128)S(1)} %get-tuple-element.8, f32[4096,512]{1,0:T(8,128)} %all-gather.2.cloned.1.call-done), kind=kOutput, calls=%fused_computation | convolution fusion | flops 3222274048 | bytes 17301504 | tf_op jit(solution)/shard_map/dot_general | solution.py:16
  (40 shorter events, 0.5 us)
Async XLA Ops:
  7.2 30.7 %copy-start = (f32[256,128]{1,0:T(8,128)S(1)}, f32[256,128]{1,0:T(8,128)}, u32[]{:S(2)}) copy-start(f32[256,128]{1,0:T(8,128)} %ri_ref.1) | copy-start | bytes 393220
  7.2 119.9 %all-gather.2.cloned.1.call-start = ((), (), s32[]{:S(2)}) async-start(), calls=%async_computation | async-start | bytes 8519680 | tf_op jit(solution)/shard_map/all_gather | solution.py:206
  23.7 6.7 %collective-permute-start.2 = (f32[96,512]{1,0:T(8,128)S(1)}, f32[96,512]{1,0:T(8,128)S(1)}, u32[]{:S(2)}, u32[]{:S(2)}) collective-permute-start(f32[96,512]{1,0:T(8,128)S(1)} %pad_maximum_fusion.4), channel_id=1, source_target_pairs={{0,1},{1,2},{2,3},{3,0},{4,5},{5,6},{6,7},{7,4},{8,9},{9,10},{10,1... | collective-permute-start | bytes 589832 | tf_op jit(solution)/shard_map/ppermute | solution.py:197
  25.9 11.1 %collective-permute-start.1 = (f32[96,512]{1,0:T(8,128)S(1)}, f32[96,512]{1,0:T(8,128)S(1)}, u32[]{:S(2)}, u32[]{:S(2)}) collective-permute-start(f32[96,512]{1,0:T(8,128)S(1)} %pad_maximum_fusion.3), channel_id=1, source_target_pairs={{0,2},{1,3},{2,0},{3,1},{4,6},{5,7},{6,4},{7,5},{8,10},{9,11},{10,... | collective-permute-start | bytes 589832 | tf_op jit(solution)/shard_map/ppermute | solution.py:197
  28.6 8.4 %collective-permute-start = (f32[96,512]{1,0:T(8,128)S(1)}, f32[96,512]{1,0:T(8,128)S(1)}, u32[]{:S(2)}, u32[]{:S(2)}) collective-permute-start(f32[96,512]{1,0:T(8,128)S(1)} %pad_maximum_fusion.2), channel_id=1, source_target_pairs={{0,3},{1,0},{2,1},{3,2},{4,7},{5,4},{6,5},{7,6},{8,11},{9,8},{10,9... | collective-permute-start | bytes 589832 | tf_op jit(solution)/shard_map/ppermute | solution.py:197
  37.8 48.2 %copy-start.1 = (f32[64,512]{1,0:T(8,128)S(1)}, f32[64,512]{1,0:T(8,128)}, u32[]{:S(2)}) copy-start(f32[64,512]{1,0:T(8,128)} %pad_maximum_fusion.6) | copy-start | bytes 393220
  38.0 5.1 %collective-permute-start.5 = (f32[2,128,128]{2,1,0:T(8,128)S(1)}, f32[2,128,128]{2,1,0:T(8,128)S(1)}, u32[]{:S(2)}, u32[]{:S(2)}) collective-permute-start(f32[2,128,128]{2,1,0:T(8,128)S(1)} %bitcast.59), channel_id=1, source_target_pairs={{0,64},{4,68},{8,72},{12,76},{16,80},{20,84},{24,88},{28,92},{32,9... | collective-permute-start | bytes 393224 | tf_op jit(solution)/shard_map/ppermute | solution.py:223
  39.3 6.9 %collective-permute-start.4 = (f32[2,128,128]{2,1,0:T(8,128)S(1)}, f32[2,128,128]{2,1,0:T(8,128)S(1)}, u32[]{:S(2)}, u32[]{:S(2)}) collective-permute-start(f32[2,128,128]{2,1,0:T(8,128)S(1)} %bitcast.60), channel_id=1, source_target_pairs={{0,128},{4,132},{8,136},{12,140},{16,144},{20,148},{24,152},{28,15... | collective-permute-start | bytes 393224 | tf_op jit(solution)/shard_map/ppermute | solution.py:223
  41.7 5.1 %collective-permute-start.3 = (f32[2,128,128]{2,1,0:T(8,128)S(1)}, f32[2,128,128]{2,1,0:T(8,128)S(1)}, u32[]{:S(2)}, u32[]{:S(2)}) collective-permute-start(f32[2,128,128]{2,1,0:T(8,128)S(1)} %bitcast.61), channel_id=1, source_target_pairs={{0,192},{4,196},{8,200},{12,204},{16,208},{20,212},{24,216},{28,22... | collective-permute-start | bytes 393224 | tf_op jit(solution)/shard_map/ppermute | solution.py:223
  46.8 10.6 %collective-permute-start.8 = (f32[2,128,128]{2,1,0:T(8,128)S(1)}, f32[2,128,128]{2,1,0:T(8,128)S(1)}, u32[]{:S(2)}, u32[]{:S(2)}) collective-permute-start(f32[2,128,128]{2,1,0:T(8,128)S(1)} %pad_maximum_fusion.8), channel_id=1, source_target_pairs={{0,16},{4,20},{8,24},{12,28},{16,32},{20,36},{24,40},{28,44},{32,4... | collective-permute-start | bytes 393224 | tf_op jit(solution)/shard_map/ppermute | solution.py:223
  49.9 12.8 %collective-permute-start.7 = (f32[2,128,128]{2,1,0:T(8,128)S(1)}, f32[2,128,128]{2,1,0:T(8,128)S(1)}, u32[]{:S(2)}, u32[]{:S(2)}) collective-permute-start(f32[2,128,128]{2,1,0:T(8,128)S(1)} %pad_maximum_fusion.8), channel_id=1, source_target_pairs={{0,32},{4,36},{8,40},{12,44},{16,48},{20,52},{24,56},{28,60},{32,0... | collective-permute-start | bytes 393224 | tf_op jit(solution)/shard_map/ppermute | solution.py:223
  55.0 12.2 %collective-permute-start.6 = (f32[2,128,128]{2,1,0:T(8,128)S(1)}, f32[2,128,128]{2,1,0:T(8,128)S(1)}, u32[]{:S(2)}, u32[]{:S(2)}) collective-permute-start(f32[2,128,128]{2,1,0:T(8,128)S(1)} %pad_maximum_fusion.8), channel_id=1, source_target_pairs={{0,48},{4,52},{8,56},{12,60},{16,0},{20,4},{24,8},{28,12},{32,16},... | collective-permute-start | bytes 393224 | tf_op jit(solution)/shard_map/ppermute | solution.py:223
  67.2 4.9 %collective-permute-start.9 = (f32[2,128,128]{2,1,0:T(8,128)S(1)}, f32[2,128,128]{2,1,0:T(8,128)S(1)}, u32[]{:S(2)}, u32[]{:S(2)}) collective-permute-start(f32[2,128,128]{2,1,0:T(8,128)S(1)} %pad_maximum_fusion.9), channel_id=1, source_target_pairs={{0,8},{4,12},{8,0},{12,4},{16,24},{20,28},{24,16},{28,20},{32,40},... | collective-permute-start | bytes 393224 | tf_op jit(solution)/shard_map/ppermute | solution.py:230
  72.2 7.4 %collective-permute-start.12 = (f32[2,2,64,128]{3,2,1,0:T(8,128)S(1)}, f32[2,2,64,128]{3,2,1,0:T(8,128)S(1)}, u32[]{:S(2)}, u32[]{:S(2)}) collective-permute-start(f32[2,2,64,128]{3,2,1,0:T(8,128)S(1)} %fusion.2), channel_id=1, source_target_pairs={{0,1},{1,2},{2,3},{3,0},{4,5},{5,6},{6,7},{7,4},{8,9},{9,10},{10,1... | collective-permute-start | bytes 393224 | tf_op jit(solution)/shard_map/ppermute | solution.py:234
  74.9 7.8 %collective-permute-start.11 = (f32[2,2,64,128]{3,2,1,0:T(8,128)S(1)}, f32[2,2,64,128]{3,2,1,0:T(8,128)S(1)}, u32[]{:S(2)}, u32[]{:S(2)}) collective-permute-start(f32[2,2,64,128]{3,2,1,0:T(8,128)S(1)} %fusion.2), channel_id=1, source_target_pairs={{0,2},{1,3},{2,0},{3,1},{4,6},{5,7},{6,4},{7,5},{8,10},{9,11},{10,... | collective-permute-start | bytes 393224 | tf_op jit(solution)/shard_map/ppermute | solution.py:234
  78.4 4.9 %collective-permute-start.10 = (f32[2,2,64,128]{3,2,1,0:T(8,128)S(1)}, f32[2,2,64,128]{3,2,1,0:T(8,128)S(1)}, u32[]{:S(2)}, u32[]{:S(2)}) collective-permute-start(f32[2,2,64,128]{3,2,1,0:T(8,128)S(1)} %fusion.2), channel_id=1, source_target_pairs={{0,3},{1,0},{2,1},{3,2},{4,7},{5,4},{6,5},{7,6},{8,11},{9,8},{10,9... | collective-permute-start | bytes 393224 | tf_op jit(solution)/shard_map/ppermute | solution.py:234
  83.5 12.0 %collective-permute-start.13 = (f32[5,2,2,64,128]{4,3,2,1,0:T(8,128)S(1)}, f32[5,2,2,64,128]{4,3,2,1,0:T(8,128)S(1)}, u32[]{:S(2)}, u32[]{:S(2)}) collective-permute-start(f32[5,2,2,64,128]{4,3,2,1,0:T(8,128)S(1)} %fusion.8), channel_id=1, source_target_pairs={{0,4},{4,0},{8,12},{12,8},{16,20},{20,16},{24,28},{28,24},{32,36},... | collective-permute-start | bytes 1966088 | tf_op jit(solution)/shard_map/ppermute | solution.py:237
  86.0 6.5 %collective-permute-start.16 = (f32[64,512]{1,0:T(8,128)S(1)}, f32[64,512]{1,0:T(8,128)S(1)}, u32[]{:S(2)}, u32[]{:S(2)}) collective-permute-start(f32[64,512]{1,0:T(8,128)S(1)} %copy-done.1), channel_id=1, source_target_pairs={{0,1},{1,2},{2,3},{3,0},{4,5},{5,6},{6,7},{7,4},{8,9},{9,10},{10,1... | collective-permute-start | bytes 393224 | tf_op jit(solution)/shard_map/ppermute | solution.py:244
  86.0 9.4 %collective-permute-start.15 = (f32[64,512]{1,0:T(8,128)S(1)}, f32[64,512]{1,0:T(8,128)S(1)}, u32[]{:S(2)}, u32[]{:S(2)}) collective-permute-start(f32[64,512]{1,0:T(8,128)S(1)} %copy-done.1), channel_id=1, source_target_pairs={{0,2},{1,3},{2,0},{3,1},{4,6},{5,7},{6,4},{7,5},{8,10},{9,11},{10,... | collective-permute-start | bytes 393224 | tf_op jit(solution)/shard_map/ppermute | solution.py:244
  89.0 6.4 %collective-permute-start.14 = (f32[64,512]{1,0:T(8,128)S(1)}, f32[64,512]{1,0:T(8,128)S(1)}, u32[]{:S(2)}, u32[]{:S(2)}) collective-permute-start(f32[64,512]{1,0:T(8,128)S(1)} %copy-done.1), channel_id=1, source_target_pairs={{0,3},{1,0},{2,1},{3,2},{4,7},{5,4},{6,5},{7,6},{8,11},{9,8},{10,9... | collective-permute-start | bytes 393224 | tf_op jit(solution)/shard_map/ppermute | solution.py:244
Sparse Core Ops, SparseCore 0:
  37.9 89.0 all-gather.1

commit v2 on v1

--- a/solution.py
+++ b/solution.py
@@ -90,7 +90,7 @@
             left[g], right[g] = left[g] - sl, right[g] - sr
 
 
-def factor_kernel(a_ref, p_ref, rc_ref, ri_ref, f_ref, w_ref, y_ref, r_ref, a, v, d, x):
+def inverse_kernel(a_ref, v, a, d, x):
     size = a.shape[0]
     tiles = size // SIDE
     a[...] = a_ref[...]
@@ -102,6 +102,7 @@
         d[...] = a[pl.ds(at, SIDE), pl.ds(at, SIDE)]
         tile_inverse(d, x)
         for step in range(tiles):
+
             @pl.when(k == step)
             def _():
                 lo, hi = step * SIDE, (step + 1) * SIDE
@@ -114,34 +115,147 @@
                     a[hi:, hi:] = a[hi:, hi:] - dot_nt(below, below)
                     v[hi:, :hi] = v[hi:, :hi] - dot_nn(below, v[lo:hi, :hi])
 
-    f = dot_nt(p_ref[...], v[...])
+
+def inverse_call(a):
+    size = a.shape[0]
+    return pl.pallas_call(
+        inverse_kernel,
+        out_shape=jax.ShapeDtypeStruct((size, size), jnp.float32),
+        scratch_shapes=[
+            pltpu.VMEM((size, size), jnp.float32),
+            pltpu.VMEM((SIDE, SIDE), jnp.float32),
+            pltpu.VMEM((SIDE, SIDE), jnp.float32),
+        ],
+        cost_estimate=pl.CostEstimate(flops=20_000_000_000, bytes_accessed=2_000_000, transcendentals=0),
+        compiler_params=pltpu.CompilerParams(vmem_limit_bytes=16 * 1024 * 1024),
+        name="factor_inverse",
+    )(a)
+
+
+def apply_kernel(v_ref, p_ref, rc_ref, ri_ref, f_ref, wh_ref, wl_ref, y_ref, r_ref):
+    v = v_ref[...]
+    f = dot_nt(p_ref[...], v)
     f_ref[...] = f
-    y = dot_nn(v[...], rc_ref[...])
+    y = dot_nn(v, rc_ref[...])
     y_ref[...] = y
     r_ref[...] = ri_ref[...] - dot_nn(f, y)
-    w_ref[...] = dot_nn(f, v[...])
-
-
-def factor_call(a, p, rc, ri):
-    size, rows, right = a.shape[0], p.shape[0], rc.shape[1]
+    wh_ref[...], wl_ref[...] = halves(dot_nn(f, v))
+
+
+def halves(array):
+    high = array.astype(jnp.bfloat16)
+    return high, (array - high.astype(jnp.float32)).astype(jnp.bfloat16)
+
+
+def apply_call(v, p, rc, ri):
+    size, rows, right = v.shape[0], p.shape[0], rc.shape[1]
     f32 = jnp.float32
     return pl.pallas_call(
-        factor_kernel,
+        apply_kernel,
         out_shape=[
             jax.ShapeDtypeStruct((rows, size), f32),
-            jax.ShapeDtypeStruct((rows, size), f32),
+            jax.ShapeDtypeStruct((rows, size), jnp.bfloat16),
+            jax.ShapeDtypeStruct((rows, size), jnp.bfloat16),
             jax.ShapeDtypeStruct((size, right), f32),
             jax.ShapeDtypeStruct((rows, right), f32),
         ],
-        scratch_shapes=[
-            pltpu.VMEM((size, size), f32),
-            pltpu.VMEM((size, size), f32),
-            pltpu.VMEM((SIDE, SIDE), f32),
-            pltpu.VMEM((SIDE, SIDE), f32),
-        ],
-        compiler_params=pltpu.CompilerParams(vmem_limit_bytes=40 * 1024 * 1024),
-        name="factor",
-    )(a, p, rc, ri)
+        cost_estimate=pl.CostEstimate(flops=2_000_000_000, bytes_accessed=4_000_000, transcendentals=0),
+        compiler_params=pltpu.CompilerParams(vmem_limit_bytes=16 * 1024 * 1024),
+        name="apply_factor",
+    )(v, p, rc, ri)
+
+
+def update_kernel(k_ref, wh_ref, wl_ref, b_ref, o_ref):
+    high, low = halves(b_ref[...])
+    wh, wl = wh_ref[...], wl_ref[...]
+    total = dot_nt(wh, high, None) + dot_nt(wh, low, None) + dot_nt(wl, high, None)
+    o_ref[...] = k_ref[...] - total
+
+
+def update_call(kernel, wh, wl, across):
+    rows, cols = kernel.shape
+    size = wh.shape[1]
+    width = 512
+    return pl.pallas_call(
+        update_kernel,
+        grid=(cols // width,),
+        in_specs=[
+            pl.BlockSpec((rows, width), lambda i: (0, i)),
+            pl.BlockSpec((rows, size), lambda i: (0, 0)),
+            pl.BlockSpec((rows, size), lambda i: (0, 0)),
+            pl.BlockSpec((width, size), lambda i: (i, 0)),
+        ],
+        out_specs=pl.BlockSpec((rows, width), lambda i: (0, i)),
+        out_shape=jax.ShapeDtypeStruct((rows, cols), jnp.float32),
+        cost_estimate=pl.CostEstimate(flops=6 * rows * cols * size, bytes_accessed=16_000_000, transcendentals=0),
+        compiler_params=pltpu.CompilerParams(vmem_limit_bytes=60 * 1024 * 1024),
+        name="trailing_update",
+    )(kernel, wh, wl, across)
+
+
+def pack_kernel(order_ref, block_ref, kernel_ref, samples_ref, *rest):
+    messages, right_ref, own, sems = rest[:-3], rest[-3], rest[-2], rest[-1]
+    strata = len(messages)
+    me = lax.axis_index("cols")
+    local_cols = kernel_ref.shape[1]
+    blocks_here = strata
+    block_rows = kernel_ref.shape[0] // blocks_here
+    part_rows = block_rows // strata
+    per_place = local_cols // PW
+    copies = []
+    for k in range(PANELS):
+        at = pl.multiple_of(lax.rem(order_ref[k], per_place) * PW, PW)
+        copies.append(
+            pltpu.make_async_copy(
+                kernel_ref.at[:, pl.ds(at, PW)], own.at[:, k * PW : (k + 1) * PW], sems.at[k]
+            )
+        )
+        copies[-1].start()
+    rows_count = lax.axis_size("rows")
+
+    def start_of(stratum):
+        slot = jnp.int32(0)
+        for u in range(blocks_here):
+            slot = jnp.where(lax.div(block_ref[u], rows_count) == stratum, u, slot)
+        return slot * block_rows
+
+    starts = [start_of(lax.div(order_ref[k], per_place)) for k in range(PANELS)]
+    for k in range(PANELS):
+        right_ref[k] = samples_ref[pl.ds(pl.multiple_of(starts[k], block_rows), block_rows), :]
+    for copy in copies:
+        copy.wait()
+    for shift in range(strata):
+        to = (me + shift) & (strata - 1)
+        out = messages[shift]
+        out[:block_rows] = own[pl.ds(pl.multiple_of(start_of(to), block_rows), block_rows), :]
+        for k in range(PANELS):
+            lo = block_rows + k * part_rows
+            at = pl.multiple_of(starts[k] + to * part_rows, part_rows)
+            out[lo : lo + part_rows] = own[pl.ds(at, part_rows), :]
+
+
+def pack_call(panel_order, row_block, kernel, samples):
+    strata = lax.axis_size("cols")
+    rows, right = samples.shape
+    block_rows = rows // row_block.shape[0]
+    size = PANELS * PW
+    f32 = jnp.float32
+    message = jax.ShapeDtypeStruct((block_rows + PANELS * (block_rows // strata), size), f32)
+    *messages, picked = pl.pallas_call(
+        pack_kernel,
+        in_specs=[
+            pl.BlockSpec(memory_space=pltpu.SMEM),
+            pl.BlockSpec(memory_space=pltpu.SMEM),
+            pl.BlockSpec(memory_space=pltpu.HBM),
+            pl.BlockSpec(memory_space=pltpu.VMEM),
+        ],
+        out_shape=[message] * strata + [jax.ShapeDtypeStruct((PANELS, block_rows, right), f32)],
+        scratch_shapes=[pltpu.VMEM((rows, size), f32), pltpu.SemaphoreType.DMA((PANELS,))],
+        cost_estimate=pl.CostEstimate(flops=0, bytes_accessed=2_000_000, transcendentals=0),
+        compiler_params=pltpu.CompilerParams(vmem_limit_bytes=60 * 1024 * 1024),
+        name="pack_messages",
+    )(panel_order, row_block, kernel, samples)
+    return messages, picked
 
 
 def pick(choices, index):
@@ -160,57 +274,15 @@
     right_cols = samples.shape[1]
     part_rows = block_rows // cols_count
     chunks = PANELS * PW // SIDE
-
-    strata = row_block // rows_count
-    slots = [
-        jnp.sum(jnp.where(strata == t, jnp.arange(blocks_here, dtype=jnp.int32), 0))
-        for t in range(blocks_here)
-    ]
-    slots = jnp.stack(slots)
-    owners, x_at, z_at, own = [], [], [], []
-    for k in range(PANELS):
-        panel = panel_order[k]
-        owner = panel * PW // local_cols
-        inside = panel % (local_cols // PW)
-        owners.append(owner)
-        x_at.append(inside // 4)
-        z_at.append(inside % 4)
-        own.append(lax.dynamic_slice_in_dim(kernel, inside * PW, PW, 1))
-    own = jnp.concatenate(own, 1)
-
-    def message(to):
-        parts = [lax.dynamic_slice_in_dim(own, slots[to] * block_rows, block_rows, 0)]
-        for k in range(PANELS):
-            parts.append(
-                lax.dynamic_slice_in_dim(
-                    own, slots[owners[k]] * block_rows + to * part_rows, part_rows, 0
-                )
-            )
-        return jnp.concatenate(parts, 0)
+    per_place = local_cols // PW
+
+    owners = [lax.div(panel_order[k], per_place) for k in range(PANELS)]
+    x_at = [lax.div(lax.rem(panel_order[k], per_place), 4) for k in range(PANELS)]
+    z_at = [lax.rem(panel_order[k], 4) for k in range(PANELS)]
+    x_here, z_here = row_place >> 4, (row_place >> 2) & 3
 
     def col_ring(shift):
         return [(i, (i + shift) % cols_count) for i in range(cols_count)]
-
-    got = []
-    for shift in range(cols_count):
-        sent = message((col_place + shift) % cols_count)
-        got.append(lax.ppermute(sent, "cols", col_ring(shift)) if shift else sent)
-    mine = jnp.concatenate(
-        [
-            pick([g[:, k * PW : (k + 1) * PW] for g in got], (col_place - owners[k]) % cols_count)
-            for k in range(PANELS)
-        ],
-        1,
-    )
-    piece = mine[:block_rows]
-    across = lax.all_gather(piece, "rows", axis=0, tiled=True)
-
-    load = []
-    for k in range(PANELS):
-        share = mine[block_rows + k * part_rows : block_rows + (k + 1) * part_rows]
-        load += [share[:, c * SIDE : (c + 1) * SIDE] for c in range(chunks)]
-        load.append(lax.dynamic_slice_in_dim(samples, slots[owners[k]] * block_rows, block_rows, 0))
-    load = jnp.concatenate(load, 0).reshape(PANELS, 2 * block_rows, SIDE)
 
     def row_pairs(move):
         pairs = []
@@ -219,34 +291,62 @@
             pairs.append((r, x % 4 * 16 + z % 8 * 2 + core))
         return pairs
 
-    def spread(load, pairs_of, place, at):
-        came = [load] + [lax.ppermute(load, "rows", pairs_of(s)) for s in range(1, 4)]
-        return jnp.stack([pick([c[k] for c in came], (place - at[k]) % 4) for k in range(PANELS)])
-
-    load = spread(load, lambda s: row_pairs(lambda x, z, c: (x + s, z, c)), row_place // 16, x_at)
-    load = spread(
-        load, lambda s: row_pairs(lambda x, z, c: (x, z + 2 * s, c)), row_place % 16 // 4, z_at
+    messages, right = pack_call(panel_order, row_block, kernel, samples)
+    got = messages[:1] + [
+        lax.ppermute(messages[s], "cols", col_ring(s)) for s in range(1, cols_count)
+    ]
+    mine = jnp.concatenate(
+        [
+            pick([g[:, k * PW : (k + 1) * PW] for g in got], (col_place - owners[k]) & (cols_count - 1))
+            for k in range(PANELS)
+        ],
+        1,
+    )
+    piece = mine[:block_rows]
+    across = lax.all_gather(piece, "rows", axis=0, tiled=True)
+
+    load = []
+    for k in range(PANELS):
+        share = mine[block_rows + k * part_rows : block_rows + (k + 1) * part_rows]
+        load += [share[:, c * SIDE : (c + 1) * SIDE] for c in range(chunks)]
+        load.append(right[k])
+    load = jnp.concatenate(load, 0).reshape(PANELS, 2 * block_rows, SIDE)
+    came = [load] + [
+        lax.ppermute(load, "rows", row_pairs(lambda x, z, c: (x + s, z, c))) for s in range(1, 4)
+    ]
+    load = jnp.stack([pick([c[k] for c in came], (x_here - x_at[k]) & 3) for k in range(PANELS)])
+    piece, load = lax.optimization_barrier((piece, load))
+    spread = [lax.ppermute(piece, "cols", col_ring(s)) for s in range(1, cols_count)]
+    other = lax.ppermute(load, "rows", row_pairs(lambda x, z, c: (x, (z // 2 ^ 1) * 2 + z % 2, c)))
+    load = jnp.stack(
+        [jnp.where(z_at[k] == (z_here ^ 1), other[k], load[k]) for k in range(PANELS)]
+    )
+    *spread, load = lax.optimization_barrier((*spread, load))
+    other = lax.ppermute(load, "rows", row_pairs(lambda x, z, c: (x, (3 - z // 2) * 2 + z % 2, c)))
+    load = jnp.stack(
+        [jnp.where((z_at[k] >> 1) != (z_here >> 1), other[k], load[k]) for k in range(PANELS)]
     )
     other = lax.ppermute(load, "rows", row_pairs(lambda x, z, c: (x, z ^ 1, c)))
-    odd = row_place // 2 % 2 == 1
+    odd = (row_place & 2) != 0
     load = jnp.stack([jnp.where(odd, other, load), jnp.where(odd, load, other)])
     square, right = load[:, :, :block_rows], load[:, :, block_rows:]
     came = [square] + [lax.ppermute(square, "cols", col_ring(s)) for s in range(1, cols_count)]
-    square = [pick(came, (col_place - to) % cols_count) for to in range(cols_count)]
+    square = [pick(came, (col_place - to) & (cols_count - 1)) for to in range(cols_count)]
     load = jnp.stack(square + [right])
     other = lax.ppermute(load, "rows", row_pairs(lambda x, z, c: (x, z, c ^ 1)))
-    odd = row_place % 2 == 1
+    odd = (row_place & 1) != 0
     load = jnp.stack([jnp.where(odd, other, load), jnp.where(odd, load, other)])
     right = load[:, cols_count].transpose(2, 1, 0, 3, 4).reshape(PANELS * PW, right_cols)
     square = load[:, :cols_count].reshape(2, cols_count, 2, PANELS, chunks, part_rows, SIDE)
     square = square.transpose(3, 2, 0, 1, 5, 4, 6).reshape(PANELS * PW, PANELS * PW)
 
-    came = [piece] + [lax.ppermute(piece, "cols", col_ring(s)) for s in range(1, cols_count)]
+    came = [piece] + spread
+    strata = [lax.div(row_block[u], rows_count) for u in range(blocks_here)]
     here = jnp.concatenate(
-        [pick(came, (col_place - strata[u]) % cols_count) for u in range(blocks_here)], 0
-    )
-    factor, weights, solved, reduced = factor_call(square, here, right, samples)
-    trailing = kernel - dot_nt(weights, across, lax.Precision.HIGH)
+        [pick(came, (col_place - strata[u]) & (cols_count - 1)) for u in range(blocks_here)], 0
+    )
+    factor, high, low, solved, reduced = apply_call(inverse_call(square), here, right, samples)
+    trailing = update_call(kernel, high, low, across)
     return trailing, factor, solved, reduced
 
 

time: 148 us -> 134 us (0.905)
  matrix products: 13.9 us -> 0 us
  Pallas kernels: 26.3 us -> 39.9 us
  starting transfers between devices: 33.6 us -> 28 us
  waiting for transfers between devices: 38 us -> 32.5 us
  other arithmetic: 5.51 us -> 2.28 us
    dot_general x1 -> x0, matrix products: 13.9 us -> none  [dot_nt(): lax.dot_general(a, b, (((1,), (1,)), ((), ())), precision=precision, pref...]
    pallas_call x1 -> x4, Pallas kernels: 26.3 us -> 39.9 us  [the longest x1 22.4 us: inverse_call(): pl.pallas_call(inverse_kernel, out_shape=jax.ShapeDtypeStruct((size, size...]
    ppermute x1, starting transfers between devices: 0.09 us -> 5.08 us  [on_device(): other = lax.ppermute(load, 'rows', row_pairs(lambda x, z, c: (x, z ^ 1, c)))]
    ppermute x9 -> x8, starting transfers between devices: 21.5 us -> 16.8 us  [the longest x3 4.88 us: on_device(): lax.ppermute(load, 'rows', row_pairs(lambda x, z, c: (x + s, z, c)))]
    all_gather x1, waiting for transfers between devices: 4.34 us -> 0.01 us  [on_device(): across = lax.all_gather(piece, 'rows', axis=0, tiled=True)]
    ppermute x3, starting transfers between devices: 6.19 us -> 2.75 us  [on_device(): lax.ppermute(square, 'cols', col_ring(s))]
    another operation x3, other arithmetic: 2.68 us -> 0.03 us  [the longest x1 0.01 us: on_device(): jnp.stack([pick([c[k] for c in came], x_here - x_at[k] & 3) for k in rang...]
    unnamed x14 -> x23, local copies, waits for them, and re-layouts: 0.11 us -> 2.32 us
  transfers between devices with their start and end apart: 18 -> 17, of which waited for: 13 -> 11; matrix products, arithmetic and copies ran while one was open for 1% -> 3% of each run, Pallas kernels for 18% -> 20%
where the time goes in v2:
time: 134 us; the launch traced here: 133 us
  Pallas kernels  39.9 us (30%)
  waiting for transfers between devices  32.5 us (24%)
  starting transfers between devices  28 us (21%)
  between operations  25.4 us (19%)
  local copies, waits for them, and re-layouts  4.72 us (4%)
  other arithmetic  2.28 us (2%)
    pallas_call x1, Pallas kernels, inverse_call(): pl.pallas_call(inverse_kernel, out_shape=jax.ShapeDtypeStruct((size, size...  22.4 us
    pallas_call x1, Pallas kernels, update_call(): pl.pallas_call(update_kernel, grid=(cols // width,), in_specs=[pl.BlockSp...  10.5 us
    ppermute x3, waiting for transfers between devices, on_device(): lax.ppermute(messages[s], 'cols', col_ring(s))  7.57 us
    ppermute x3, waiting for transfers between devices, on_device(): lax.ppermute(square, 'cols', col_ring(s))  6.3 us
    ppermute x1, starting transfers between devices, on_device(): other = lax.ppermute(load, 'rows', row_pairs(lambda x, z, c: (x, z ^ 1, c)))  5.08 us
    ppermute x3, starting transfers between devices, on_device(): lax.ppermute(load, 'rows', row_pairs(lambda x, z, c: (x + s, z, c)))  4.88 us
    ppermute x3, waiting for transfers between devices, on_device(): lax.ppermute(load, 'rows', row_pairs(lambda x, z, c: (x + s, z, c)))  4.76 us
    ppermute x3, starting transfers between devices, on_device(): lax.ppermute(messages[s], 'cols', col_ring(s))  4.68 us
  transfers between devices with their start and end apart: 17, of which 11 were waited for; matrix products, arithmetic and copies ran while one was open for 3% of the time, Pallas kernels for 20%

profile of v2, /device:TPU:1, one launch (start us, length us, event | category | flops | bytes accessed | tf_op | source)
XLA Modules:
  0.0 132.9 jit_solution(11684002137973548939)
XLA Ops:
  7.2 0.0 all-gather.2.cloned.1.call-start
  7.2 2.9 %pack_messages.1 = (f32[96,512]{1,0:T(8,128)}, f32[96,512]{1,0:T(8,128)}, f32[96,512]{1,0:T(8,128)}, f32[96,512]{1,0:T(8,128)}, f32[2,64,128]{2,1,0:T(8,128)}) custom-call(s32[2]{0:T(128)} %order_ref.1, s32[4]{0:T(128)} %block_ref.1, f32[256,4096]{1,0:T(8,128)} %k_ref.1, f32[256,128]{1,0:T(8,128)} %ri_ref.1), custom_call_target="tpu_custom_call" | custom-call | bytes 2000000 | tf_op jit(solution)/shard_map/pack_messages/pallas_call | solution.py:244
  10.1 3.6 %collective-permute-start = (f32[96,512]{1,0:T(8,128)}, f32[96,512]{1,0:T(8,128)S(1)}, u32[]{:S(2)}, u32[]{:S(2)}) collective-permute-start(f32[96,512]{1,0:T(8,128)} %get-tuple-element.20), channel_id=1, source_target_pairs={{0,3},{1,0},{2,1},{3,2},{4,7},{5,4},{6,5},{7,6},{8,11},{9,8},{10,9... | collective-permute-start | bytes 589832 | tf_op jit(solution)/shard_map/ppermute | solution.py:296
  13.8 0.3 collective-permute-start.1
  14.1 0.7 collective-permute-start.2
  14.8 0.6 fusion.14
  19.0 3.0 %collective-permute-done = f32[96,512]{1,0:T(8,128)S(1)} collective-permute-done((f32[96,512]{1,0:T(8,128)}, f32[96,512]{1,0:T(8,128)S(1)}, u32[]{:S(2)}, u32[]{:S(2)}) %collective-permute-start) | collective-permute-done | bytes 196640 | tf_op jit(solution)/shard_map/ppermute | solution.py:296
  22.0 0.0 collective-permute-done.1
  22.0 4.5 %collective-permute-done.2 = f32[96,512]{1,0:T(8,128)S(1)} collective-permute-done((f32[96,512]{1,0:T(8,128)}, f32[96,512]{1,0:T(8,128)S(1)}, u32[]{:S(2)}, u32[]{:S(2)}) %collective-permute-start.2) | collective-permute-done | bytes 196640 | tf_op jit(solution)/shard_map/ppermute | solution.py:296
  26.5 1.0 fusion.8
  27.5 0.7 pad_maximum_fusion.3
  28.2 0.0 all-gather.2.cloned.1.call-update
  28.3 0.8 constant_dynamic-update-slice_fusion.5
  29.1 0.8 constant_dynamic-update-slice_fusion.10
  29.9 1.3 collective-permute-start.5
  31.2 2.5 %collective-permute-start.4 = (f32[2,128,128]{2,1,0:T(8,128)S(1)}, f32[2,128,128]{2,1,0:T(8,128)S(1)}, u32[]{:S(2)}, u32[]{:S(2)}) collective-permute-start(f32[2,128,128]{2,1,0:T(8,128)S(1)} %bitcast.54), channel_id=1, source_target_pairs={{0,128},{4,132},{8,136},{12,140},{16,144},{20,148},{24,152},{28,15... | collective-permute-start | bytes 393224 | tf_op jit(solution)/shard_map/ppermute | solution.py:315
  33.6 1.2 collective-permute-start.3
  34.8 1.0 collective-permute-done.5
  35.7 3.8 %collective-permute-done.4 = f32[2,128,128]{2,1,0:T(8,128)S(1)} collective-permute-done((f32[2,128,128]{2,1,0:T(8,128)S(1)}, f32[2,128,128]{2,1,0:T(8,128)S(1)}, u32[]{:S(2)}, u32[]{:S(2)}) %collective-permute-start.4) | collective-permute-done | bytes 131104 | tf_op jit(solution)/shard_map/ppermute | solution.py:315
  39.6 3.1 %collective-permute-start.9 = (f32[2,128,128]{2,1,0:T(8,128)S(1)}, f32[2,128,128]{2,1,0:T(8,128)S(1)}, u32[]{:S(2)}, u32[]{:S(2)}) collective-permute-start(f32[2,128,128]{2,1,0:T(8,128)S(1)} %pad_maximum_fusion.4), channel_id=1, source_target_pairs={{0,16},{4,20},{8,24},{12,28},{16,0},{20,4},{24,8},{28,12},{32,48},... | collective-permute-start | bytes 393224 | tf_op jit(solution)/shard_map/ppermute | solution.py:320
  42.7 0.0 collective-permute-start.8
  42.7 0.3 collective-permute-start.7
  43.0 1.1 collective-permute-start.6
  44.1 2.7 %collective-permute-done.9 = f32[2,128,128]{2,1,0:T(8,128)S(1)} collective-permute-done((f32[2,128,128]{2,1,0:T(8,128)S(1)}, f32[2,128,128]{2,1,0:T(8,128)S(1)}, u32[]{:S(2)}, u32[]{:S(2)}) %collective-permute-start.9) | collective-permute-done | bytes 131104 | tf_op jit(solution)/shard_map/ppermute | solution.py:320
  46.9 0.1 collective-permute-done.8
  47.0 1.3 collective-permute-done.7
  48.2 2.5 %collective-permute-done.6 = f32[64,512]{1,0:T(8,128)S(1)} collective-permute-done((f32[64,512]{1,0:T(8,128)}, f32[64,512]{1,0:T(8,128)S(1)}, u32[]{:S(2)}, u32[]{:S(2)}) %collective-permute-start.6) | collective-permute-done | bytes 131104 | tf_op jit(solution)/shard_map/ppermute | solution.py:319
  50.7 4.2 %collective-permute-start.10 = (f32[2,128,128]{2,1,0:T(8,128)S(1)}, f32[2,128,128]{2,1,0:T(8,128)S(1)}, u32[]{:S(2)}, u32[]{:S(2)}) collective-permute-start(f32[2,128,128]{2,1,0:T(8,128)S(1)} %pad_maximum_fusion.5), channel_id=1, source_target_pairs={{0,48},{4,52},{8,56},{12,60},{16,32},{20,36},{24,40},{28,44},{32,1... | collective-permute-start | bytes 393224 | tf_op jit(solution)/shard_map/ppermute | solution.py:325
  54.9 3.8 %collective-permute-done.10 = f32[2,128,128]{2,1,0:T(8,128)S(1)} collective-permute-done((f32[2,128,128]{2,1,0:T(8,128)S(1)}, f32[2,128,128]{2,1,0:T(8,128)S(1)}, u32[]{:S(2)}, u32[]{:S(2)}) %collective-permute-start.10) | collective-permute-done | bytes 131104 | tf_op jit(solution)/shard_map/ppermute | solution.py:325
  58.8 5.1 %collective-permute-start.11 = (f32[2,128,128]{2,1,0:T(8,128)S(1)}, f32[2,128,128]{2,1,0:T(8,128)S(1)}, u32[]{:S(2)}, u32[]{:S(2)}) collective-permute-start(f32[2,128,128]{2,1,0:T(8,128)S(1)} %pad_maximum_fusion.6), channel_id=1, source_target_pairs={{0,8},{4,12},{8,0},{12,4},{16,24},{20,28},{24,16},{28,20},{32,40},... | collective-permute-start | bytes 393224 | tf_op jit(solution)/shard_map/ppermute | solution.py:329
  63.9 3.5 %collective-permute-done.11 = f32[2,128,128]{2,1,0:T(8,128)S(1)} collective-permute-done((f32[2,128,128]{2,1,0:T(8,128)S(1)}, f32[2,128,128]{2,1,0:T(8,128)S(1)}, u32[]{:S(2)}, u32[]{:S(2)}) %collective-permute-start.11) | collective-permute-done | bytes 131104 | tf_op jit(solution)/shard_map/ppermute | solution.py:329
  67.4 0.1 collective-permute-start.14
  67.5 1.3 collective-permute-start.13
  68.8 1.4 %collective-permute-start.12 = (f32[2,2,64,128]{3,2,1,0:T(8,128)S(1)}, f32[2,2,64,128]{3,2,1,0:T(8,128)S(1)}, u32[]{:S(2)}, u32[]{:S(2)}) collective-permute-start(f32[2,2,64,128]{3,2,1,0:T(8,128)S(1)} %fusion.2), channel_id=1, source_target_pairs={{0,3},{1,0},{2,1},{3,2},{4,7},{5,4},{6,5},{7,6},{8,11},{9,8},{10,9... | collective-permute-start | bytes 393224 | tf_op jit(solution)/shard_map/ppermute | solution.py:333
  70.2 6.3 %collective-permute-done.14 = f32[2,2,64,128]{3,2,1,0:T(8,128)S(1)} collective-permute-done((f32[2,2,64,128]{3,2,1,0:T(8,128)S(1)}, f32[2,2,64,128]{3,2,1,0:T(8,128)S(1)}, u32[]{:S(2)}, u32[]{:S(2)}) %collective-permute-start.14) | collective-permute-done | bytes 131104 | tf_op jit(solution)/shard_map/ppermute | solution.py:333
  76.7 1.8 %collective-permute-start.15 = (f32[5,2,2,64,128]{4,3,2,1,0:T(8,128)S(1)}, f32[5,2,2,64,128]{4,3,2,1,0:T(8,128)S(1)}, u32[]{:S(2)}, u32[]{:S(2)}) collective-permute-start(f32[5,2,2,64,128]{4,3,2,1,0:T(8,128)S(1)} %fusion.4), channel_id=1, source_target_pairs={{0,4},{4,0},{8,12},{12,8},{16,20},{20,16},{24,28},{28,24},{32,36},... | collective-permute-start | bytes 1966088 | tf_op jit(solution)/shard_map/ppermute | solution.py:336
  78.5 0.6 fusion.13
  86.7 0.1 select_select_fusion.3
  86.8 0.1 select_bitcast_fusion
  86.9 0.1 fusion
  87.0 0.4 copy.8
  87.5 0.1 copy.12
  87.6 0.0 copy-start.2
  87.6 22.4 %factor_inverse.1.v_ref = f32[512,512]{1,0:T(8,128)S(1)} custom-call(f32[512,512]{1,0:T(8,128)S(1)} %bitcast.49), custom_call_target="tpu_custom_call" | custom-call | flops 20000000000 | bytes 2000000 | tf_op jit(solution)/shard_map/factor_inverse/pallas_call | solution.py:121
  110.0 4.1 %apply_factor.1 = (f32[256,512]{1,0:T(8,128)}, bf16[256,512]{1,0:T(8,128)(2,1)S(1)}, bf16[256,512]{1,0:T(8,128)(2,1)S(1)}, f32[512,128]{1,0:T(8,128)}, f32[256,128]{1,0:T(8,128)}) custom-call(f32[512,512]{1,0:T(8,128)S(1)} %factor_inverse.1.v_ref, f32[256,512]{1,0:T(8,128)S(1)} %pad_maximum_fusion.p_ref, f32[512,128]{1,0:T(8,128)S(1)} %bitcast.50, ...), custom_call_target="tpu_custom_call" | custom-call | flops 2000000000 | bytes 4000000 | tf_op jit(solution)/shard_map/apply_factor/pallas_call | solution.py:153
  114.1 0.7 copy-done
  114.8 0.7 copy-done.1
  115.5 10.5 %trailing_update.1 = f32[256,4096]{1,0:T(8,128)} custom-call(f32[256,4096]{1,0:T(8,128)} %k_ref.1, bf16[256,512]{1,0:T(8,128)(2,1)} %copy-done, bf16[256,512]{1,0:T(8,128)(2,1)} %copy-done.1, f32[4096,512]{1,0:T(8,128)} %all-gather.2.cloned.1.call-done.b_ref), custom_call_target="tpu_custom_call" | custom-call | flops 3221225472 | bytes 16000000 | tf_op jit(solution)/shard_map/trailing_update/pallas_call | solution.py:179
  (39 shorter events, 0.4 us)
Async XLA Ops:
  7.2 7.7 %copy-start.5 = (s32[2]{0:T(128)S(1)}, s32[2]{0:T(128)}, u32[]{:S(2)}) copy-start(s32[2]{0:T(128)} %order_ref.1) | copy-start | bytes 28
  7.2 108.4 %all-gather.2.cloned.1.call-start = ((), (), s32[]{:S(2)}) async-start(), calls=%async_computation | async-start | bytes 8519680 | tf_op jit(solution)/shard_map/all_gather | solution.py:306
  10.1 11.9 %collective-permute-start = (f32[96,512]{1,0:T(8,128)}, f32[96,512]{1,0:T(8,128)S(1)}, u32[]{:S(2)}, u32[]{:S(2)}) collective-permute-start(f32[96,512]{1,0:T(8,128)} %get-tuple-element.20), channel_id=1, source_target_pairs={{0,3},{1,0},{2,1},{3,2},{4,7},{5,4},{6,5},{7,6},{8,11},{9,8},{10,9... | collective-permute-start | bytes 589832 | tf_op jit(solution)/shard_map/ppermute | solution.py:296
  13.8 8.2 %collective-permute-start.1 = (f32[96,512]{1,0:T(8,128)}, f32[96,512]{1,0:T(8,128)S(1)}, u32[]{:S(2)}, u32[]{:S(2)}) collective-permute-start(f32[96,512]{1,0:T(8,128)} %get-tuple-element.21), channel_id=1, source_target_pairs={{0,2},{1,3},{2,0},{3,1},{4,6},{5,7},{6,4},{7,5},{8,10},{9,11},{10,... | collective-permute-start | bytes 589832 | tf_op jit(solution)/shard_map/ppermute | solution.py:296
  14.1 12.4 %collective-permute-start.2 = (f32[96,512]{1,0:T(8,128)}, f32[96,512]{1,0:T(8,128)S(1)}, u32[]{:S(2)}, u32[]{:S(2)}) collective-permute-start(f32[96,512]{1,0:T(8,128)} %get-tuple-element.22), channel_id=1, source_target_pairs={{0,1},{1,2},{2,3},{3,0},{4,5},{5,6},{6,7},{7,4},{8,9},{9,10},{10,1... | collective-permute-start | bytes 589832 | tf_op jit(solution)/shard_map/ppermute | solution.py:296
  26.5 52.0 %copy-start.4 = (s32[4]{0:T(128)S(1)}, s32[4]{0:T(128)}, u32[]{:S(2)}) copy-start(s32[4]{0:T(128)} %block_ref.1) | copy-start | bytes 52
  28.2 58.4 %copy-start.3 = (f32[64,512]{1,0:T(8,128)S(1)}, f32[64,512]{1,0:T(8,128)}, u32[]{:S(2)}) copy-start(f32[64,512]{1,0:T(8,128)} %pad_maximum_fusion.3) | copy-start | bytes 393220
  29.9 5.9 %collective-permute-start.5 = (f32[2,128,128]{2,1,0:T(8,128)S(1)}, f32[2,128,128]{2,1,0:T(8,128)S(1)}, u32[]{:S(2)}, u32[]{:S(2)}) collective-permute-start(f32[2,128,128]{2,1,0:T(8,128)S(1)} %bitcast.53), channel_id=1, source_target_pairs={{0,64},{4,68},{8,72},{12,76},{16,80},{20,84},{24,88},{28,92},{32,9... | collective-permute-start | bytes 393224 | tf_op jit(solution)/shard_map/ppermute | solution.py:315
  31.2 8.4 %collective-permute-start.4 = (f32[2,128,128]{2,1,0:T(8,128)S(1)}, f32[2,128,128]{2,1,0:T(8,128)S(1)}, u32[]{:S(2)}, u32[]{:S(2)}) collective-permute-start(f32[2,128,128]{2,1,0:T(8,128)S(1)} %bitcast.54), channel_id=1, source_target_pairs={{0,128},{4,132},{8,136},{12,140},{16,144},{20,148},{24,152},{28,15... | collective-permute-start | bytes 393224 | tf_op jit(solution)/shard_map/ppermute | solution.py:315
  33.6 5.9 %collective-permute-start.3 = (f32[2,128,128]{2,1,0:T(8,128)S(1)}, f32[2,128,128]{2,1,0:T(8,128)S(1)}, u32[]{:S(2)}, u32[]{:S(2)}) collective-permute-start(f32[2,128,128]{2,1,0:T(8,128)S(1)} %bitcast.55), channel_id=1, source_target_pairs={{0,192},{4,196},{8,200},{12,204},{16,208},{20,212},{24,216},{28,22... | collective-permute-start | bytes 393224 | tf_op jit(solution)/shard_map/ppermute | solution.py:315
  39.6 7.3 %collective-permute-start.9 = (f32[2,128,128]{2,1,0:T(8,128)S(1)}, f32[2,128,128]{2,1,0:T(8,128)S(1)}, u32[]{:S(2)}, u32[]{:S(2)}) collective-permute-start(f32[2,128,128]{2,1,0:T(8,128)S(1)} %pad_maximum_fusion.4), channel_id=1, source_target_pairs={{0,16},{4,20},{8,24},{12,28},{16,0},{20,4},{24,8},{28,12},{32,48},... | collective-permute-start | bytes 393224 | tf_op jit(solution)/shard_map/ppermute | solution.py:320
  42.7 4.3 %collective-permute-start.8 = (f32[64,512]{1,0:T(8,128)}, f32[64,512]{1,0:T(8,128)S(1)}, u32[]{:S(2)}, u32[]{:S(2)}) collective-permute-start(f32[64,512]{1,0:T(8,128)} %pad_maximum_fusion.3), channel_id=1, source_target_pairs={{0,3},{1,0},{2,1},{3,2},{4,7},{5,4},{6,5},{7,6},{8,11},{9,8},{10,9... | collective-permute-start | bytes 393224 | tf_op jit(solution)/shard_map/ppermute | solution.py:319
  42.7 5.6 %collective-permute-start.7 = (f32[64,512]{1,0:T(8,128)}, f32[64,512]{1,0:T(8,128)S(1)}, u32[]{:S(2)}, u32[]{:S(2)}) collective-permute-start(f32[64,512]{1,0:T(8,128)} %pad_maximum_fusion.3), channel_id=1, source_target_pairs={{0,2},{1,3},{2,0},{3,1},{4,6},{5,7},{6,4},{7,5},{8,10},{9,11},{10,... | collective-permute-start | bytes 393224 | tf_op jit(solution)/shard_map/ppermute | solution.py:319
  43.0 7.7 %collective-permute-start.6 = (f32[64,512]{1,0:T(8,128)}, f32[64,512]{1,0:T(8,128)S(1)}, u32[]{:S(2)}, u32[]{:S(2)}) collective-permute-start(f32[64,512]{1,0:T(8,128)} %pad_maximum_fusion.3), channel_id=1, source_target_pairs={{0,1},{1,2},{2,3},{3,0},{4,5},{5,6},{6,7},{7,4},{8,9},{9,10},{10,1... | collective-permute-start | bytes 393224 | tf_op jit(solution)/shard_map/ppermute | solution.py:319
  50.7 8.0 %collective-permute-start.10 = (f32[2,128,128]{2,1,0:T(8,128)S(1)}, f32[2,128,128]{2,1,0:T(8,128)S(1)}, u32[]{:S(2)}, u32[]{:S(2)}) collective-permute-start(f32[2,128,128]{2,1,0:T(8,128)S(1)} %pad_maximum_fusion.5), channel_id=1, source_target_pairs={{0,48},{4,52},{8,56},{12,60},{16,32},{20,36},{24,40},{28,44},{32,1... | collective-permute-start | bytes 393224 | tf_op jit(solution)/shard_map/ppermute | solution.py:325
  58.8 8.6 %collective-permute-start.11 = (f32[2,128,128]{2,1,0:T(8,128)S(1)}, f32[2,128,128]{2,1,0:T(8,128)S(1)}, u32[]{:S(2)}, u32[]{:S(2)}) collective-permute-start(f32[2,128,128]{2,1,0:T(8,128)S(1)} %pad_maximum_fusion.6), channel_id=1, source_target_pairs={{0,8},{4,12},{8,0},{12,4},{16,24},{20,28},{24,16},{28,20},{32,40},... | collective-permute-start | bytes 393224 | tf_op jit(solution)/shard_map/ppermute | solution.py:329
  67.4 9.0 %collective-permute-start.14 = (f32[2,2,64,128]{3,2,1,0:T(8,128)S(1)}, f32[2,2,64,128]{3,2,1,0:T(8,128)S(1)}, u32[]{:S(2)}, u32[]{:S(2)}) collective-permute-start(f32[2,2,64,128]{3,2,1,0:T(8,128)S(1)} %fusion.2), channel_id=1, source_target_pairs={{0,1},{1,2},{2,3},{3,0},{4,5},{5,6},{6,7},{7,4},{8,9},{9,10},{10,1... | collective-permute-start | bytes 393224 | tf_op jit(solution)/shard_map/ppermute | solution.py:333
  67.5 9.0 %collective-permute-start.13 = (f32[2,2,64,128]{3,2,1,0:T(8,128)S(1)}, f32[2,2,64,128]{3,2,1,0:T(8,128)S(1)}, u32[]{:S(2)}, u32[]{:S(2)}) collective-permute-start(f32[2,2,64,128]{3,2,1,0:T(8,128)S(1)} %fusion.2), channel_id=1, source_target_pairs={{0,2},{1,3},{2,0},{3,1},{4,6},{5,7},{6,4},{7,5},{8,10},{9,11},{10,... | collective-permute-start | bytes 393224 | tf_op jit(solution)/shard_map/ppermute | solution.py:333
  68.8 7.7 %collective-permute-start.12 = (f32[2,2,64,128]{3,2,1,0:T(8,128)S(1)}, f32[2,2,64,128]{3,2,1,0:T(8,128)S(1)}, u32[]{:S(2)}, u32[]{:S(2)}) collective-permute-start(f32[2,2,64,128]{3,2,1,0:T(8,128)S(1)} %fusion.2), channel_id=1, source_target_pairs={{0,3},{1,0},{2,1},{3,2},{4,7},{5,4},{6,5},{7,6},{8,11},{9,8},{10,9... | collective-permute-start | bytes 393224 | tf_op jit(solution)/shard_map/ppermute | solution.py:333
  76.7 10.1 %collective-permute-start.15 = (f32[5,2,2,64,128]{4,3,2,1,0:T(8,128)S(1)}, f32[5,2,2,64,128]{4,3,2,1,0:T(8,128)S(1)}, u32[]{:S(2)}, u32[]{:S(2)}) collective-permute-start(f32[5,2,2,64,128]{4,3,2,1,0:T(8,128)S(1)} %fusion.4), channel_id=1, source_target_pairs={{0,4},{4,0},{8,12},{12,8},{16,20},{20,16},{24,28},{28,24},{32,36},... | collective-permute-start | bytes 1966088 | tf_op jit(solution)/shard_map/ppermute | solution.py:336
  87.6 22.4 %copy-start.2 = (f32[256,128]{1,0:T(8,128)S(1)}, f32[256,128]{1,0:T(8,128)}, u32[]{:S(2)}) copy-start(f32[256,128]{1,0:T(8,128)} %ri_ref.1) | copy-start | bytes 393220
  114.1 0.7 copy-start
  114.8 0.7 copy-start.1
Sparse Core Ops, SparseCore 0:
  28.4 85.5 all-gather.1
